TPU v7x, 512 devices: a whole 4x4x16 slice. The times are simulated.
512 devices in a mesh: group: 64 (over z, x), pair: 8 (over y, core).
Axes of the slice: x: 4, y: 4, z: 16, core: 2. Of those that a mesh axis runs over, the one named last changes fastest.
Arguments:
- embeddings: bfloat16 [32768, 4096], P(('group', 'pair')), may hold values from -6 to 6
- dest: int32 [32768, 1], replicated, may hold values from 0 to 63; in each aligned block of 64 rows (0 to 63, 64 to 127, ...) at most 2 rows name the same one
- labels: int32 [64, 8], P('group'), may hold values from 0 to 4, never falling along the last dimension, each value on 1 to 2 neighbouring positions
Outputs:
- smoothed: bfloat16 [32768, 4096], P(('group', 'pair'))
Inputs may be any that keep to these rules, and one draw needn't show every extreme that they name: `dest`: in each aligned block of 64 rows (one source cell) at most 2 documents name one owner group, and exactly 2 for some. `labels`: each row is non-falling along pair, with 5 clusters of one or two consecutive blocks.
All inputs are finite; a program needn't handle non-finite values.
Results may differ from a plain program's by a relative error of at most 0.0075.
Values may be sent and summed in bfloat16 or wider, within the bound.
A program may use at most 64 MiB of HBM per device.

v0:
```python
import math

import jax
import jax.numpy as jnp
from jax import lax
from jax.sharding import PartitionSpec as P

score_scale = 64.0
self_weight = math.exp(4.0)
along_rows = (((1,), (1,)), ((), ()))
along_cols = (((0,), (0,)), ((), ()))


def shifted(block, axis, distance):
    devices = range(lax.axis_size(axis))
    route = [(i - distance, i) for i in devices if i - distance in devices]
    return lax.ppermute(block, axis, route)


def normalized(rows):
    values = rows.astype(jnp.float32)
    factor = lax.rsqrt(jnp.mean(values * values, axis=-1, keepdims=True) + 1e-05)
    return (values * factor * (1.0 / math.sqrt(values.shape[-1]))).astype(jnp.bfloat16)


def live_slots(routes, source_pair, owner, capacity):
    column = lax.dynamic_index_in_dim(routes, source_pair, axis=1, keepdims=False)
    counts = jnp.sum((column == owner).astype(jnp.int32), axis=1)
    return (
        (jnp.arange(capacity, dtype=jnp.int32)[None, :] < counts[:, None])
        .reshape(-1)
        .astype(jnp.float32)
    )


def pair_weights(left, right, mask):
    scores = lax.dot_general(left, right, along_rows, preferred_element_type=jnp.float32)
    return jnp.exp(score_scale * scores) * mask


def on_device(embeddings, dest, labels):
    groups = lax.axis_size("group")
    pairs = lax.axis_size("pair")
    group_at = lax.axis_index("group")
    pair_at = lax.axis_index("pair")
    count = embeddings.shape[0]
    width = embeddings.shape[1]
    capacity = 2 * count // groups
    slots = groups * capacity
    routes = dest.reshape(groups, pairs, count)
    own_routes = lax.dynamic_index_in_dim(
        lax.dynamic_index_in_dim(routes, group_at, axis=0, keepdims=False),
        pair_at,
        axis=0,
        keepdims=False,
    )
    hits = (own_routes[:, None] == jnp.arange(groups, dtype=jnp.int32)[None, :]).astype(jnp.int32)
    ranks = jnp.sum(jnp.cumsum(hits, axis=0) * hits, axis=1) - 1
    slot = own_routes * capacity + ranks
    match = (slot[None, :] == jnp.arange(slots, dtype=jnp.int32)[:, None]).astype(jnp.int32)
    slot_doc = jnp.sum(match * jnp.arange(count, dtype=jnp.int32)[None, :], axis=1)
    filled = jnp.sum(match, axis=1)
    hat = normalized(embeddings)
    outgoing = jnp.where(filled[:, None] > 0, hat[slot_doc], jnp.zeros((), jnp.bfloat16))
    arrived = lax.all_to_all(
        outgoing.reshape(groups, capacity, width), "group", split_axis=0, concat_axis=0, tiled=True
    )
    block = arrived.reshape(slots, width)
    marks = labels[0]
    mine = marks[pair_at]
    live_mine = live_slots(routes, pair_at, group_at, capacity)
    next_at = jnp.minimum(pair_at + 1, pairs - 1)
    joined_next = jnp.logical_and(pair_at + 1 < pairs, marks[next_at] == mine).astype(jnp.float32)
    live_next = live_slots(routes, next_at, group_at, capacity)
    apart = (jnp.arange(slots)[:, None] != jnp.arange(slots)[None, :]).astype(jnp.float32)
    own_weights = pair_weights(block, block, live_mine[None, :] * apart)
    numer = self_weight * block.astype(jnp.float32) + jnp.dot(
        own_weights.astype(jnp.bfloat16), block, preferred_element_type=jnp.float32
    )
    denom = self_weight + jnp.sum(own_weights, axis=1)
    neighbour = shifted(block, "pair", -1)
    next_weights = pair_weights(
        block, neighbour, live_mine[:, None] * live_next[None, :] * joined_next
    )
    next_rounded = next_weights.astype(jnp.bfloat16)
    numer = numer + jnp.dot(next_rounded, neighbour, preferred_element_type=jnp.float32)
    denom = denom + jnp.sum(next_weights, axis=1)
    column_numer = lax.dot_general(
        next_rounded, block, along_cols, preferred_element_type=jnp.float32
    )
    column_denom = jnp.sum(next_weights, axis=0)
    came_numer, came_denom = (
        shifted(column_numer.astype(jnp.bfloat16), "pair", 1).astype(column_numer.dtype),
        shifted(column_denom.astype(jnp.bfloat16), "pair", 1).astype(column_denom.dtype),
    )
    numer = numer + came_numer
    denom = denom + came_denom
    block_out = (math.sqrt(width) * numer / denom[:, None]).astype(jnp.bfloat16)
    returned = lax.all_to_all(
        block_out.reshape(groups, capacity, width), "group", split_axis=0, concat_axis=0, tiled=True
    )
    return returned.reshape(slots, width)[slot]


def solution(mesh):
    in_specs = (P(("group", "pair"), None), P(), P("group", None))
    out_specs = P(("group", "pair"), None)
    return jax.shard_map(
        on_device, mesh=mesh, in_specs=in_specs, out_specs=out_specs, check_vma=False
    )
```

profile of v0, /device:TPU:10, one launch (start us, length us, event | category | flops | bytes accessed | tf_op | source)
XLA Modules:
  0.0 179.0 jit_solution(6090410284316539274)
XLA Ops:
  0.0 1.2 fusion.8
  1.3 0.5 broadcast.123
  1.8 1.9 %reduce.5 = s32[32768]{0:T(1024)S(1)} reduce(s32[32768,1]{0,1:T(1,128)} %param.4, s32[]{:T(128)} %broadcast.123), dimensions={1}, to_apply=%param.4.reduce_sub_computation.3 | reduce | bytes 262148 | tf_op args[1]
  4.4 1.2 fusion.10
  5.7 1.2 gather_fusion
  6.9 0.7 gather.9
  7.6 1.0 broadcast_select_fusion
  8.6 73.6 %all_to_all.10 = bf16[64,2,4096]{2,1,0:T(2,128)(2,1)S(1)} all-to-all(bf16[64,2,4096]{2,1,0:T(2,128)(2,1)S(1)} %broadcast_select_fusion), channel_id=1, replica_groups=mesh['group'=64,'pair'=8] {'group'}, dimensions={0} | all-to-all | bytes 2097152 | tf_op jit(solution)/shard_map/all_to_all | solution.py:65
  82.6 1.9 %collective-permute-start = (bf16[128,4096]{1,0:T(8,128)(2,1)S(1)}, bf16[128,4096]{1,0:T(8,128)(2,1)S(1)}, u32[]{:S(2)}, u32[]{:S(2)}) collective-permute-start(bf16[128,4096]{1,0:T(8,128)(2,1)S(1)} %reshape.150), channel_id=1, source_target_pairs={{1,0},{2,1},{3,2},{4,3},{5,4},{6,5},{7,6},{9,8},{10,9},{11,10},{12... | collective-permute-start | bytes 3145736 | tf_op jit(solution)/shard_map/ppermute | solution.py:17
  84.6 0.7 constant_dynamic-slice_fusion
  86.6 2.4 %fusion.12 = (s32[64]{0:T(128)S(1)}, s32[64]{0:T(128)S(1)}) fusion(s32[64,8,64]{2,1,0:T(8,128)S(1)} %reshape.149, s32[]{:T(128)S(6)} %select_n.50, s32[]{:T(128)S(6)} %axis_index.23, s32[]{:T(128)S(6)} %select_n.46), kind=kLoop, calls=%fused_computation.25 | loop fusion | flops 24448 | bytes 33292 | tf_op jit(solution)/shard_map/reduce_sum | solution.py:28
  89.3 7.5 %collective-permute-done = bf16[128,4096]{1,0:T(8,128)(2,1)S(1)} collective-permute-done((bf16[128,4096]{1,0:T(8,128)(2,1)S(1)}, bf16[128,4096]{1,0:T(8,128)(2,1)S(1)}, u32[]{:S(2)}, u32[]{:S(2)}) %collective-permute-start) | collective-permute-done | bytes 1048608 | tf_op jit(solution)/shard_map/ppermute | solution.py:17
  96.9 0.5 fusion.21
  97.4 0.4 convolution_convert_fusion
  97.8 3.8 %collective-permute-start.1 = (bf16[128,4096]{1,0:T(8,128)(2,1)S(1)}, bf16[128,4096]{1,0:T(8,128)(2,1)S(1)}, u32[]{:S(2)}, u32[]{:S(2)}) collective-permute-start(bf16[128,4096]{1,0:T(8,128)(2,1)S(1)} %convolution_convert_fusion), channel_id=1, source_target_pairs={{0,1},{1,2},{2,3},{3,4},{4,5},{5,6},{6,7},{8,9},{9,10},{10,11},{11... | collective-permute-start | bytes 3145736 | tf_op jit(solution)/shard_map/ppermute | solution.py:17
  101.6 0.5 fusion.22
  102.0 1.9 %collective-permute-start.2 = (bf16[128]{0:T(256)(128)(2,1)S(1)}, bf16[128]{0:T(256)(128)(2,1)S(1)}, u32[]{:S(2)}, u32[]{:S(2)}) collective-permute-start(bf16[128]{0:T(256)(128)(2,1)S(1)} %get-tuple-element.8), channel_id=1, source_target_pairs={{0,1},{1,2},{2,3},{3,4},{4,5},{5,6},{6,7},{8,9},{9,10},{10,11},{11... | collective-permute-start | bytes 776 | tf_op jit(solution)/shard_map/ppermute | solution.py:17
  104.0 0.5 convolution_add_fusion.1
  104.4 9.7 %collective-permute-done.2 = bf16[128]{0:T(256)(128)(2,1)S(1)} collective-permute-done((bf16[128]{0:T(256)(128)(2,1)S(1)}, bf16[128]{0:T(256)(128)(2,1)S(1)}, u32[]{:S(2)}, u32[]{:S(2)}) %collective-permute-start.2) | collective-permute-done | bytes 288 | tf_op jit(solution)/shard_map/ppermute | solution.py:17
  114.2 0.7 fusion.3
  114.9 1.5 reshape.151
  116.4 5.9 %all-to-all-start.1 = ((bf16[64,2,4096]{2,1,0:T(2,128)(2,1)}), bf16[64,2,4096]{2,1,0:T(2,128)(2,1)S(1)}, u32[]{:S(2)}, u32[]{:S(2)}) async-start(bf16[64,2,4096]{2,1,0:T(2,128)(2,1)} %reshape.151), calls=%async_computation.1 | async-start | bytes 2097152 | tf_op jit(solution)/shard_map/all_to_all | solution.py:99
  122.4 54.5 %all-to-all-done.1 = bf16[64,2,4096]{2,1,0:T(2,128)(2,1)S(1)} async-done(((bf16[64,2,4096]{2,1,0:T(2,128)(2,1)}), bf16[64,2,4096]{2,1,0:T(2,128)(2,1)S(1)}, u32[]{:S(2)}, u32[]{:S(2)}) %all-to-all-start.1) | async-done | bytes 1048608 | tf_op jit(solution)/shard_map/all_to_all | solution.py:99
  177.3 1.7 gather_fusion.1
  (23 shorter events, 2.0 us)
Async XLA Ops:
  8.6 76.0 %copy-start = (s32[1,8]{1,0:T(1,128)S(1)}, s32[1,8]{1,0:T(1,128)}, u32[]{:S(2)}) copy-start(s32[1,8]{1,0:T(1,128)} %param.5) | copy-start | bytes 100
  82.6 14.2 %collective-permute-start = (bf16[128,4096]{1,0:T(8,128)(2,1)S(1)}, bf16[128,4096]{1,0:T(8,128)(2,1)S(1)}, u32[]{:S(2)}, u32[]{:S(2)}) collective-permute-start(bf16[128,4096]{1,0:T(8,128)(2,1)S(1)} %reshape.150), channel_id=1, source_target_pairs={{1,0},{2,1},{3,2},{4,3},{5,4},{6,5},{7,6},{9,8},{10,9},{11,10},{12... | collective-permute-start | bytes 3145736 | tf_op jit(solution)/shard_map/ppermute | solution.py:17
  97.8 16.4 %collective-permute-start.1 = (bf16[128,4096]{1,0:T(8,128)(2,1)S(1)}, bf16[128,4096]{1,0:T(8,128)(2,1)S(1)}, u32[]{:S(2)}, u32[]{:S(2)}) collective-permute-start(bf16[128,4096]{1,0:T(8,128)(2,1)S(1)} %convolution_convert_fusion), channel_id=1, source_target_pairs={{0,1},{1,2},{2,3},{3,4},{4,5},{5,6},{6,7},{8,9},{9,10},{10,11},{11... | collective-permute-start | bytes 3145736 | tf_op jit(solution)/shard_map/ppermute | solution.py:17
  102.0 12.1 %collective-permute-start.2 = (bf16[128]{0:T(256)(128)(2,1)S(1)}, bf16[128]{0:T(256)(128)(2,1)S(1)}, u32[]{:S(2)}, u32[]{:S(2)}) collective-permute-start(bf16[128]{0:T(256)(128)(2,1)S(1)} %get-tuple-element.8), channel_id=1, source_target_pairs={{0,1},{1,2},{2,3},{3,4},{4,5},{5,6},{6,7},{8,9},{9,10},{10,11},{11... | collective-permute-start | bytes 776 | tf_op jit(solution)/shard_map/ppermute | solution.py:17
  116.4 60.5 %all-to-all-start.1 = ((bf16[64,2,4096]{2,1,0:T(2,128)(2,1)}), bf16[64,2,4096]{2,1,0:T(2,128)(2,1)S(1)}, u32[]{:S(2)}, u32[]{:S(2)}) async-start(bf16[64,2,4096]{2,1,0:T(2,128)(2,1)} %reshape.151), calls=%async_computation.1 | async-start | bytes 2097152 | tf_op jit(solution)/shard_map/all_to_all | solution.py:99
where the time goes:
time: 179 us
  blocking collectives  73.6 us (41%)
  waiting for transfers between devices  71.7 us (40%)
  starting transfers between devices  13.6 us (8%)
  other arithmetic  8.28 us (5%)
  local copies, waits for them, and re-layouts  7.65 us (4%)
  matrix products  2.55 us (1%)
    all_to_all x1, blocking collectives, on_device(): lax.all_to_all(outgoing.reshape(groups, capacity, width), 'group', split_...  73.6 us
    all_to_all x1, waiting for transfers between devices, on_device(): lax.all_to_all(block_out.reshape(groups, capacity, width), 'group', split...  54.5 us
    ppermute x3, waiting for transfers between devices, shifted(): return lax.ppermute(block, axis, route)  17.2 us
    ppermute x3, starting transfers between devices, shifted(): return lax.ppermute(block, axis, route)  7.6 us
    all_to_all x1, starting transfers between devices, on_device(): lax.all_to_all(block_out.reshape(groups, capacity, width), 'group', split...  5.95 us
  transfers between devices with their start and end apart: 4, of which 3 were waited for; matrix products, arithmetic and copies ran while one was open for 2% of the time, Pallas kernels for 0%

commit v1 on v0

--- a/solution.py
+++ b/solution.py
@@ -3,6 +3,8 @@
 import jax
 import jax.numpy as jnp
 from jax import lax
+from jax.experimental import pallas as pl
+from jax.experimental.pallas import tpu as pltpu
 from jax.sharding import PartitionSpec as P
 
 score_scale = 64.0
@@ -38,7 +40,7 @@
     return jnp.exp(score_scale * scores) * mask
 
 
-def on_device(embeddings, dest, labels):
+def padded(embeddings, dest, labels):
     groups = lax.axis_size("group")
     pairs = lax.axis_size("pair")
     group_at = lax.axis_index("group")
@@ -102,6 +104,512 @@
     return returned.reshape(slots, width)[slot]
 
 
+ZS, XS, PAIRS, COUNT, WIDTH = 16, 4, 8, 64, 4096
+GROUPS = ZS * XS
+SLOTS = XS + 1
+SUB, LANE = 16, 256
+BLOCK = GROUPS * 2
+SENT = ZS * SLOTS
+BATCH = 2
+BATCHES = ZS // BATCH
+MESH = pl.DeviceIdType.MESH
+f32, bf16, i32 = jnp.float32, jnp.bfloat16, jnp.int32
+
+
+def distance_at(t):
+    half = t // 2
+    far = jnp.where(t % 2 == 0, 8 - half, 8 + half)
+    return jnp.where(t == 0, 0, far)
+
+
+def step_of(distance):
+    near = jnp.where(distance < 8, 16 - 2 * distance, 2 * distance - 15)
+    return jnp.where(distance == 0, 0, near)
+
+
+def mirror(t):
+    return jnp.where(t < 2, t, jnp.where(t % 2 == 0, t + 1, t - 1))
+
+
+def iota(shape, axis):
+    return lax.broadcasted_iota(i32, shape, axis)
+
+
+def compact_kernel(
+    x_ref, dest_ref, lab_ref, out_ref, ok_ref,
+    hat, wide, zsend, zland, own, beside, rows, outd, zback, cand, zret,
+    mark, marks, counts, place, pick, unpick, sides, lives, choice, weights,
+    lab_x_send, lab_x_recv, lab_z_send, lab_z_recv, z_send, z_recv, x_send, x_recv, y_send, y_recv,
+    xb_send, xb_recv, zb_send, zb_recv,
+):
+    group = lax.axis_index("group")
+    pair = lax.axis_index("pair")
+    z, x = group // XS, group % XS
+
+    def at(zz, xx):
+        return (zz * XS + xx, pair)
+
+    def z_peer(t):
+        return lax.rem(z + distance_at(t), ZS)
+
+    def x_peer(j):
+        return lax.rem(x + j, XS)
+
+    def pair_peer(side):
+        return lax.rem(pair + jnp.where(side == 0, 1, PAIRS - 1), PAIRS)
+
+    barrier = pltpu.get_barrier_semaphore()
+    for d in range(1, ZS):
+        pl.semaphore_signal(barrier, inc=1, device_id=at(lax.rem(z + d, ZS), x), device_id_type=MESH)
+    for j in range(1, XS):
+        pl.semaphore_signal(barrier, inc=1, device_id=at(z, x_peer(j)), device_id_type=MESH)
+    for step in (1, PAIRS - 1):
+        pl.semaphore_signal(
+            barrier, inc=1, device_id=(group, lax.rem(pair + step, PAIRS)), device_id_type=MESH
+        )
+
+    @pl.loop(0, COUNT // 16)
+    def _(i):
+        r = pl.ds(pl.multiple_of(i * 16, 16), 16)
+        values = x_ref[r, :].astype(f32)
+        factor = lax.rsqrt(jnp.mean(values * values, axis=-1, keepdims=True) + 1e-05)
+        hat[r, :] = (values * factor * (1.0 / math.sqrt(WIDTH))).astype(bf16)
+
+    turned = dest_ref[...].T
+    for parity in range(2):
+        part = turned[parity * COUNT : (parity + 1) * COUNT, :]
+        unit = jnp.left_shift(jnp.ones_like(part), (part & 7) * 4)
+        for k in range(GROUPS // 8):
+            held = jnp.sum(jnp.where((part >> 3) == k, unit, 0), axis=0, keepdims=True)
+            nibble = jnp.broadcast_to(held, (8, 256)) >> (iota((8, 256), 0) * 4)
+            counts[parity, 8 * k : 8 * k + 8, :] = (nibble & 3).astype(f32)
+    second = [(counts[parity] == 2.0).astype(f32) for parity in range(2)]
+    both = (second[0] + second[1]).astype(bf16)
+    need_col = jnp.sum(second[0] + second[1], axis=1, keepdims=True)
+    need_row = lax.dot_general(
+        jnp.ones((8, 256), bf16), both, along_rows, preferred_element_type=f32
+    )[0:1, :]
+    g_col, g_row = iota((GROUPS, GROUPS), 0), iota((GROUPS, GROUPS), 1)
+    ahead = jnp.logical_or(
+        need_row > need_col, jnp.logical_and(need_row == need_col, g_row < g_col)
+    )
+    standing = jnp.sum(ahead.astype(i32), axis=1, keepdims=True)
+    position = (standing % ZS) * XS + standing // ZS
+    place[...] = jnp.broadcast_to(position, (GROUPS, 128))
+
+    cell = group * (PAIRS // 2) + pair // 2
+    line = dest_ref[pl.ds(cell, 1), :]
+    lane = iota((1, 128), 1)
+    mine = lane // COUNT == pair % 2
+    line = jnp.where(mine, line, -1)
+    eye = iota((128, 128), 0) == iota((128, 128), 1)
+    line_col = jnp.sum(jnp.where(eye, jnp.broadcast_to(line, (128, 128)), 0), axis=1, keepdims=True)
+    earlier = jnp.logical_and(line_col == line, iota((128, 128), 0) < iota((128, 128), 1))
+    rank = jnp.sum(earlier.astype(i32), axis=0, keepdims=True)
+    spot = jnp.sum(
+        jnp.where(iota((GROUPS, 128), 0) == line, place[...], 0), axis=0, keepdims=True
+    )
+    step = step_of((spot // XS - z + ZS) % ZS)
+    slot = step * SLOTS + jnp.where(rank == 0, spot % XS, XS)
+    slot = jnp.where(mine, slot, -1)
+    fold = slot[:, :COUNT] + slot[:, COUNT:] + 1
+    slot_col = jnp.sum(
+        jnp.where(
+            iota((COUNT, COUNT), 0) == iota((COUNT, COUNT), 1),
+            jnp.broadcast_to(fold, (COUNT, COUNT)),
+            0,
+        ),
+        axis=1,
+        keepdims=True,
+    )
+    pick[...] = (iota((SENT, COUNT), 0) == fold).astype(f32).astype(bf16)
+    unpick[...] = (iota((COUNT, SENT), 1) == slot_col).astype(f32).astype(bf16)
+
+    @pl.loop(0, SUB)
+    def _(c):
+        got = jnp.dot(
+            pick[...],
+            hat[:, pl.ds(pl.multiple_of(c * LANE, LANE), LANE)],
+            preferred_element_type=f32,
+        )
+        spread(wide, c, SENT, got)
+
+    mark[...] = jnp.zeros((1, 128), i32)
+    mark[:, 0:PAIRS] = lab_ref[...]
+    marks[pl.ds(group, 1), :, :] = mark[...].reshape(1, 1, 128)
+    zland[0] = docs_of(wide, 0, SLOTS)
+
+    pl.semaphore_wait(barrier, ZS - 1 + XS - 1 + 2)
+
+    def lab_x(j):
+        here = marks.at[pl.ds(group, 1)]
+        return pltpu.make_async_remote_copy(
+            here, here, lab_x_send.at[j], lab_x_recv.at[j],
+            device_id=at(z, x_peer(j)), device_id_type=MESH,
+        )
+
+    def lab_z(t):
+        here = marks.at[pl.ds(z * XS, XS)]
+        return pltpu.make_async_remote_copy(
+            here, here, lab_z_send.at[t], lab_z_recv.at[mirror(t)],
+            device_id=at(z_peer(t), x), device_id_type=MESH,
+        )
+
+    def lab_z_arrival(t):
+        there = marks.at[pl.ds(z_peer(t) * XS, XS)]
+        return pltpu.make_async_remote_copy(
+            there, there, lab_z_send.at[t], lab_z_recv.at[t],
+            device_id=at(z_peer(t), x), device_id_type=MESH,
+        )
+
+    def lab_x_arrival(j):
+        there = marks.at[pl.ds(z * XS + lax.rem(x + XS - j, XS), 1)]
+        return pltpu.make_async_remote_copy(
+            there, there, lab_x_send.at[j], lab_x_recv.at[j],
+            device_id=at(z, x_peer(j)), device_id_type=MESH,
+        )
+
+    def z_out(t):
+        return pltpu.make_async_remote_copy(
+            zsend.at[t], zland.at[mirror(t)], z_send.at[t], z_recv.at[mirror(t)],
+            device_id=at(z_peer(t), x), device_id_type=MESH,
+        )
+
+    def z_in(t):
+        return pltpu.make_async_remote_copy(
+            zsend.at[t], zland.at[t], z_send.at[t], z_recv.at[t],
+            device_id=at(z_peer(t), x), device_id_type=MESH,
+        )
+
+    for j in range(1, XS):
+        lab_x(j).start()
+
+    @pl.loop(1, ZS)
+    def _(t):
+        zsend[t] = docs_of(wide, t * SLOTS, SLOTS)
+        z_out(t).start()
+
+    for j in range(1, XS):
+        lab_x_arrival(j).wait_recv()
+
+    @pl.loop(1, ZS)
+    def _(t):
+        lab_z(t).start()
+
+    here = place[:, 0:1] == group
+    held = [
+        jnp.sum(jnp.where(here, counts[parity], 0.0), axis=0, keepdims=True) for parity in range(2)
+    ]
+    s_lane = iota((256, BLOCK), 1)
+    s_source = lax.rem(z + distance_at(s_lane // (2 * XS)), ZS) * XS + (s_lane // 2) % XS
+    for n, shift in enumerate((0, PAIRS - 1, 1)):
+        other = lax.rem(pair + shift, PAIRS)
+        row = jnp.where(other % 2 == 0, held[0], held[1])
+        chosen = (iota((256, BLOCK), 0) == s_source * (PAIRS // 2) + other // 2).astype(f32)
+        filled = jnp.dot(
+            jnp.broadcast_to(row, (8, 256)).astype(bf16), chosen.astype(bf16),
+            preferred_element_type=f32,
+        )
+        lives[n] = (filled > (iota((8, BLOCK), 1) % 2).astype(f32)).astype(f32)
+
+    at_here = (place[:, 0:GROUPS] == z * XS + iota((GROUPS, GROUPS), 1) % XS).astype(f32)
+    wanted = jnp.where(
+        pair % 2 == 0, (counts[0] == 2.0).astype(f32), (counts[1] == 2.0).astype(f32)
+    )
+    owner_of = lax.dot_general(
+        at_here.astype(bf16), wanted.astype(bf16), along_cols, preferred_element_type=f32
+    )
+    t_row = iota((GROUPS, 256), 0) // XS
+    c_row = (lax.rem(z + distance_at(t_row), ZS) * XS + x) * (PAIRS // 2) + pair // 2
+    choice[...] = jnp.broadcast_to(
+        jnp.sum(jnp.where(iota((GROUPS, 256), 1) == c_row, owner_of, 0.0), axis=1, keepdims=True),
+        (GROUPS, 128),
+    )
+
+    plane = (place[:, 0:ZS] // XS == iota((GROUPS, ZS), 1)).astype(f32).astype(bf16)
+    most = jnp.zeros((1, 1), f32)
+    for parity in range(2):
+        load = lax.dot_general(
+            plane, (counts[parity] == 2.0).astype(f32).astype(bf16), along_cols,
+            preferred_element_type=f32,
+        )
+        most = jnp.maximum(most, jnp.max(jnp.max(load, axis=1, keepdims=True), axis=0, keepdims=True))
+    ok_ref[...] = jnp.broadcast_to((most < 1.5).astype(i32), (8, 128))
+
+    @pl.loop(1, ZS)
+    def _(t):
+        lab_z_arrival(t).wait_recv()
+
+    def add_marks(g, total):
+        return total + jnp.where(place[pl.ds(g, 1), :] == group, marks[g], 0)
+
+    label = lax.fori_loop(0, GROUPS, add_marks, jnp.zeros((1, 128), i32))
+
+    def label_at(q):
+        return jnp.sum(jnp.where(lane == q, label, 0), axis=1, keepdims=True)
+
+    joined_prev = jnp.logical_and(label_at(pair - 1) == label_at(pair), pair > 0)
+    joined_next = jnp.logical_and(label_at(pair + 1) == label_at(pair), pair < PAIRS - 1)
+    sides[0] = jnp.broadcast_to(joined_prev.astype(f32), (8, 128))
+    sides[1] = jnp.broadcast_to(joined_next.astype(f32), (8, 128))
+
+    def x_out(b, j, kind):
+        two = pl.ds(b * BATCH, BATCH)
+        to = x_peer(j)
+        source = zland.at[two, XS if kind else to]
+        return pltpu.make_async_remote_copy(
+            source, own.at[two, x, kind], x_send.at[b, j, kind], x_recv.at[b, j, kind],
+            device_id=at(z, to), device_id_type=MESH,
+        )
+
+    def y_out(b, side):
+        two = pl.ds(b * BATCH, BATCH)
+        return pltpu.make_async_remote_copy(
+            own.at[two], beside.at[side, two], y_send.at[b, side], y_recv.at[b, side],
+            device_id=(group, pair_peer(side)), device_id_type=MESH,
+        )
+
+    def own_docs(b):
+        return own[pl.ds(b * BATCH, BATCH)].reshape(16, SUB, LANE)
+
+    @pl.loop(0, BATCHES + 2)
+    def _(s):
+        @pl.when(s < BATCHES)
+        def _():
+            b = s
+
+            @pl.when(b > 0)
+            def _():
+                z_in(2 * b).wait_recv()
+
+            z_in(2 * b + 1).wait_recv()
+            for j in range(1, XS):
+                for kind in range(2):
+                    x_out(b, j, kind).start()
+            for k in range(BATCH):
+                own[b * BATCH + k, x, 0] = zland[b * BATCH + k, x]
+                own[b * BATCH + k, x, 1] = zland[b * BATCH + k, XS]
+
+        @pl.when(jnp.logical_and(s >= 1, s <= BATCHES))
+        def _():
+            b = s - 1
+            for j in range(1, XS):
+                for kind in range(2):
+                    x_out(b, j, kind).wait_recv()
+            for side in range(2):
+                y_out(b, side).start()
+            put_wide(wide, 0, own_docs(b))
+
+            @pl.loop(0, SUB)
+            def _(c):
+                rows[c, pl.ds(pl.multiple_of(b * 16, 16), 16), :] = gather(wide, c, 16).astype(bf16)
+
+        @pl.when(s >= 2)
+        def _():
+            b = s - 2
+            for side in range(2):
+                y_out(b, side).wait_recv()
+            two = pl.ds(b * BATCH, BATCH)
+            use_prev = jnp.broadcast_to(sides[0][0:1, :], (8, 128)) > 0.5
+            use_prev = jnp.concatenate([use_prev[0:1].astype(f32)] * 2, axis=1)
+            prev = beside[0, two].reshape(16 * SUB, LANE).astype(f32)
+            nxt = beside[1, two].reshape(16 * SUB, LANE).astype(f32)
+            chosen = jnp.where(jnp.broadcast_to(use_prev, (16 * SUB, LANE)) > 0.5, prev, nxt)
+            put_wide(wide, 0, chosen.reshape(16, SUB, LANE))
+
+            @pl.loop(0, SUB)
+            def _(c):
+                rows[c, pl.ds(pl.multiple_of(BLOCK + b * 16, 16), 16), :] = gather(wide, c, 16).astype(bf16)
+
+    def add_scores(c, total):
+        both_rows = rows[c]
+        return total + lax.dot_general(
+            both_rows[:BLOCK], both_rows, along_rows, preferred_element_type=f32
+        )
+
+    scores = lax.fori_loop(0, SUB, add_scores, jnp.zeros((BLOCK, 2 * BLOCK), f32))
+    apart = (iota((BLOCK, BLOCK), 0) != iota((BLOCK, BLOCK), 1)).astype(f32)
+    prev_mask = lives[1][0:1, :] * sides[0][0:1, :]
+    next_mask = lives[2][0:1, :] * sides[1][0:1, :]
+    mask = jnp.concatenate(
+        [lives[0][0:1, :] * apart, jnp.broadcast_to(prev_mask + next_mask, (BLOCK, BLOCK))], axis=1
+    )
+    raw = jnp.exp(score_scale * scores) * mask
+    weights[...] = raw.astype(bf16)
+    denom = self_weight + jnp.sum(raw, axis=1, keepdims=True)
+    scale = jnp.broadcast_to(math.sqrt(WIDTH) / denom, (BLOCK, LANE))
+
+    @pl.loop(0, SUB)
+    def _(c):
+        both_rows = rows[c]
+        numer = self_weight * both_rows[:BLOCK].astype(f32) + jnp.dot(
+            weights[...], both_rows, preferred_element_type=f32
+        )
+        spread(wide, c, BLOCK, numer * scale)
+
+    def x_back(b, j, kind):
+        two = pl.ds(b * BATCH, BATCH)
+        to = x_peer(j)
+        target = cand.at[two, x] if kind else zback.at[two, x]
+        return pltpu.make_async_remote_copy(
+            outd.at[two, to, kind], target, xb_send.at[b, j, kind], xb_recv.at[b, j, kind],
+            device_id=at(z, to), device_id_type=MESH,
+        )
+
+    def z_home(t):
+        return pltpu.make_async_remote_copy(
+            zback.at[t], zret.at[mirror(t)], zb_send.at[t], zb_recv.at[mirror(t)],
+            device_id=at(z_peer(t), x), device_id_type=MESH,
+        )
+
+    def z_arrival(t):
+        return pltpu.make_async_remote_copy(
+            zback.at[t], zret.at[t], zb_send.at[t], zb_recv.at[t],
+            device_id=at(z_peer(t), x), device_id_type=MESH,
+        )
+
+    def choose(t):
+        chosen = cand[t, XS - 1]
+        for k in range(XS - 1):
+            flag = choice[pl.ds(t * XS + k, 1), :]
+            flag = jnp.broadcast_to(jnp.concatenate([flag, flag], axis=1), (SUB, LANE))
+            chosen = jnp.where(flag > 0.5, cand[t, k].astype(f32), chosen.astype(f32)).astype(bf16)
+        zback[t, XS] = chosen
+
+    @pl.loop(0, BATCHES + 1)
+    def _(s):
+        @pl.when(s < BATCHES)
+        def _():
+            b = s
+            for k in range(BATCH):
+                t = b * BATCH + k
+                outd[t] = docs_of(wide, t * 2 * XS, 2 * XS).reshape(XS, 2, SUB, LANE)
+            for j in range(1, XS):
+                for kind in range(2):
+                    x_back(b, j, kind).start()
+            for k in range(BATCH):
+                t = b * BATCH + k
+                zback[t, x] = outd[t, x, 0]
+                cand[t, x] = outd[t, x, 1]
+
+        @pl.when(s >= 1)
+        def _():
+            b = s - 1
+            for j in range(1, XS):
+                for kind in range(2):
+                    x_back(b, j, kind).wait_recv()
+            for k in range(BATCH):
+                choose(b * BATCH + k)
+
+            @pl.when(b > 0)
+            def _():
+                z_home(2 * b).start()
+
+            z_home(2 * b + 1).start()
+
+    put_wide(wide, 0, zback[0])
+
+    @pl.loop(1, ZS)
+    def _(t):
+        z_arrival(t).wait_recv()
+        put_wide(wide, t * SLOTS, zret[t])
+
+    @pl.loop(0, SUB)
+    def _(c):
+        got = gather(wide, c, SENT).astype(bf16)
+        out_ref[:, pl.ds(pl.multiple_of(c * LANE, LANE), LANE)] = jnp.dot(
+            unpick[...], got, preferred_element_type=f32
+        ).astype(bf16)
+
+    for j in range(1, XS):
+        lab_x(j).wait_send()
+
+    @pl.loop(1, ZS)
+    def _(t):
+        lab_z(t).wait_send()
+        z_out(t).wait_send()
+        z_home(t).wait_send()
+
+    @pl.loop(0, BATCHES)
+    def _(b):
+        for j in range(1, XS):
+            for kind in range(2):
+                x_out(b, j, kind).wait_send()
+                x_back(b, j, kind).wait_send()
+        for side in range(2):
+            y_out(b, side).wait_send()
+
+
+def put_wide(wide, first, docs):
+    n = docs.shape[0]
+    flat = docs.astype(f32).reshape(n * SUB, LANE)
+    for h in range(2):
+        wide[h, pl.ds(pl.multiple_of(first * SUB, SUB), n * SUB), :] = flat[:, h * 128 : (h + 1) * 128]
+
+
+def docs_of(wide, first, n):
+    at = pl.ds(pl.multiple_of(first * SUB, SUB), n * SUB)
+    flat = jnp.concatenate([wide[0, at, :], wide[1, at, :]], axis=1)
+    return flat.astype(bf16).reshape(n, SUB, LANE)
+
+
+def spread(wide, c, n, values):
+    for h in range(2):
+        wide[h, pl.ds(c, n, stride=SUB), :] = values[:, h * 128 : (h + 1) * 128]
+
+
+def gather(wide, c, n):
+    return jnp.concatenate([wide[h, pl.ds(c, n, stride=SUB), :] for h in range(2)], axis=1)
+
+
+def compact(embeddings, dest, labels):
+    vmem = pl.BlockSpec(memory_space=pltpu.VMEM)
+    dma = pltpu.SemaphoreType.DMA
+    return pl.pallas_call(
+        compact_kernel,
+        out_shape=(
+            jax.ShapeDtypeStruct((COUNT, WIDTH), bf16),
+            jax.ShapeDtypeStruct((8, 128), i32),
+        ),
+        in_specs=[vmem] * 3,
+        out_specs=(vmem, vmem),
+        scratch_shapes=[
+            pltpu.VMEM((COUNT, WIDTH), bf16),
+            pltpu.VMEM((2, BLOCK * SUB, 128), f32),
+            pltpu.VMEM((ZS, SLOTS, SUB, LANE), bf16),
+            pltpu.VMEM((ZS, SLOTS, SUB, LANE), bf16),
+            pltpu.VMEM((ZS, XS, 2, SUB, LANE), bf16),
+            pltpu.VMEM((2, ZS, XS, 2, SUB, LANE), bf16),
+            pltpu.VMEM((SUB, 2 * BLOCK, LANE), bf16),
+            pltpu.VMEM((ZS, XS, 2, SUB, LANE), bf16),
+            pltpu.VMEM((ZS, SLOTS, SUB, LANE), bf16),
+            pltpu.VMEM((ZS, XS, SUB, LANE), bf16),
+            pltpu.VMEM((ZS, SLOTS, SUB, LANE), bf16),
+            pltpu.VMEM((1, 128), i32),
+            pltpu.VMEM((GROUPS, 1, 128), i32),
+            pltpu.VMEM((2, GROUPS, 256), f32),
+            pltpu.VMEM((GROUPS, 128), i32),
+            pltpu.VMEM((SENT, COUNT), bf16),
+            pltpu.VMEM((COUNT, SENT), bf16),
+            pltpu.VMEM((2, 8, 128), f32),
+            pltpu.VMEM((3, 8, BLOCK), f32),
+            pltpu.VMEM((GROUPS, 128), f32),
+            pltpu.VMEM((BLOCK, 2 * BLOCK), bf16),
+            dma((XS,)), dma((XS,)), dma((ZS,)), dma((ZS,)), dma((ZS,)), dma((ZS,)),
+            dma((BATCHES, XS, 2)), dma((BATCHES, XS, 2)), dma((BATCHES, 2)), dma((BATCHES, 2)),
+            dma((BATCHES, XS, 2)), dma((BATCHES, XS, 2)), dma((ZS,)), dma((ZS,)),
+        ],
+        compiler_params=pltpu.CompilerParams(
+            collective_id=0, has_side_effects=True, vmem_limit_bytes=40 << 20
+        ),
+    )(embeddings, dest, labels)
+
+
+def on_device(embeddings, dest, labels):
+    out, ok = compact(embeddings, dest.reshape(GROUPS * PAIRS * COUNT // 128, 128), labels)
+    return lax.cond(ok[0, 0] == 1, lambda: out, lambda: padded(embeddings, dest, labels))
+
+
 def solution(mesh):
     in_specs = (P(("group", "pair"), None), P(), P("group", None))
     out_specs = P(("group", "pair"), None)

time: 179 us -> 128 us (0.72)
  the two profiles are of different devices: /device:TPU:10 before, /device:TPU:1 now
where the time goes in v1:
time: 128 us
  Pallas kernels  126 us (98%)
  local copies, waits for them, and re-layouts  1.31 us (1%)
    pallas_call x1, Pallas kernels, compact(): pl.pallas_call(compact_kernel, out_shape=(jax.ShapeDtypeStruct((COUNT, WI...  126 us

profile of v1, /device:TPU:1, one launch (start us, length us, event | category | flops | bytes accessed | tf_op | source)
XLA Modules:
  0.0 127.8 jit_solution(17856718894884843952)
XLA Ops:
  0.0 125.9 %shard_map.39 = (bf16[64,4096]{1,0:T(8,128)(2,1)S(1)}, s32[8,128]{1,0:T(8,128)S(1)}) custom-call(bf16[64,4096]{1,0:T(8,128)(2,1)} %x_ref.1, s32[256,128]{1,0:T(8,128)} %bitcast.29, s32[1,8]{1,0:T(1,128)} %lab_ref.1), custom_call_target="tpu_custom_call" | custom-call | tf_op jit(solution)/shard_map/pallas_call | solution.py:568
  125.9 0.5 slice.3
  127.0 0.8 copy.13
  (1 shorter events, 0.0 us)

commit v2 on v0

--- a/solution.py
+++ b/solution.py
@@ -3,6 +3,8 @@
 import jax
 import jax.numpy as jnp
 from jax import lax
+from jax.experimental import pallas as pl
+from jax.experimental.pallas import tpu as pltpu
 from jax.sharding import PartitionSpec as P
 
 score_scale = 64.0
@@ -38,7 +40,7 @@
     return jnp.exp(score_scale * scores) * mask
 
 
-def on_device(embeddings, dest, labels):
+def padded(embeddings, dest, labels):
     groups = lax.axis_size("group")
     pairs = lax.axis_size("pair")
     group_at = lax.axis_index("group")
@@ -102,6 +104,599 @@
     return returned.reshape(slots, width)[slot]
 
 
+ZS, XS, PAIRS, COUNT, WIDTH = 16, 4, 8, 64, 4096
+GROUPS = ZS * XS
+SUB, LANE = 16, 256
+BLOCK = GROUPS * 2
+SENT = GROUPS + ZS
+BATCH = 2
+BATCHES = ZS // BATCH
+QUAD = 4
+QUADS = ZS // QUAD
+AHEAD = 3
+UNROLL = 4
+MESH = pl.DeviceIdType.MESH
+f32, bf16, i32 = jnp.float32, jnp.bfloat16, jnp.int32
+
+
+def distance_at(t):
+    half = t // 2
+    far = jnp.where(t % 2 == 0, 8 - half, 8 + half)
+    return jnp.where(t == 0, 0, far)
+
+
+def step_of(distance):
+    near = jnp.where(distance < 8, 16 - 2 * distance, 2 * distance - 15)
+    return jnp.where(distance == 0, 0, near)
+
+
+def mirror(t):
+    return jnp.where(t < 2, t, jnp.where(t % 2 == 0, t + 1, t - 1))
+
+
+def iota(shape, axis):
+    return lax.broadcasted_iota(i32, shape, axis)
+
+
+def put_wide(wide, first, docs):
+    n = docs.shape[0]
+    flat = docs.astype(f32).reshape(n * SUB, LANE)
+    for h in range(2):
+        wide[h, pl.ds(pl.multiple_of(first * SUB, SUB), n * SUB), :] = flat[:, h * 128 : (h + 1) * 128]
+
+
+def docs_of(wide, first, n):
+    at = pl.ds(pl.multiple_of(first * SUB, SUB), n * SUB)
+    flat = jnp.concatenate([wide[0, at, :], wide[1, at, :]], axis=1)
+    return flat.astype(bf16).reshape(n, SUB, LANE)
+
+
+def spread(wide, c, first, n, values):
+    for h in range(2):
+        wide[h, pl.ds(first * SUB + c, n, stride=SUB), :] = values[:, h * 128 : (h + 1) * 128]
+
+
+def gather(wide, c, n):
+    return jnp.concatenate([wide[h, pl.ds(c, n, stride=SUB), :] for h in range(2)], axis=1)
+
+
+def chunk(c):
+    return pl.ds(pl.multiple_of(c * LANE, LANE), LANE)
+
+
+def compact_kernel(
+    x_ref, dest_ref, lab_ref, out_ref, ok_ref,
+    xv, hat, wide, send_r, send_s, land_s, own, beside, rows, out_r, out_s, back_s, cand, ret_r, ret_s,
+    mark, marks, counts, place, pick, unpick, sides, lives, choice, weights, scores,
+    in_sem, lab_x_send, lab_x_recv, lab_z_send, lab_z_recv,
+    r_send, r_recv, s_send, s_recv, m_send, m_recv, yr_send, yr_recv, ys_send, ys_recv,
+    rb_send, rb_recv, mb_send, mb_recv, sb_send, sb_recv,
+):
+    group = lax.axis_index("group")
+    pair = lax.axis_index("pair")
+    z, x = group // XS, group % XS
+
+    def at(zz, xx):
+        return (zz * XS + xx, pair)
+
+    def z_peer(t):
+        return lax.rem(z + distance_at(t), ZS)
+
+    def x_peer(j):
+        return lax.rem(x + j, XS)
+
+    def pair_peer(side):
+        return lax.rem(pair + jnp.where(side == 0, 1, PAIRS - 1), PAIRS)
+
+    def remote(source, target, send, recv, device):
+        return pltpu.make_async_remote_copy(
+            source, target, send, recv, device_id=device, device_id_type=MESH
+        )
+
+    barrier = pltpu.get_barrier_semaphore()
+
+    @pl.loop(1, GROUPS)
+    def _(d):
+        pl.semaphore_signal(
+            barrier, inc=1, device_id=(lax.rem(group + d, GROUPS), pair), device_id_type=MESH
+        )
+
+    for step in (1, PAIRS - 1):
+        pl.semaphore_signal(
+            barrier, inc=1, device_id=(group, lax.rem(pair + step, PAIRS)), device_id_type=MESH
+        )
+
+    load_x = pltpu.make_async_copy(x_ref, xv, in_sem)
+    load_x.start()
+
+    turned = dest_ref[...].T
+    for parity in range(2):
+        part = turned[parity * COUNT : (parity + 1) * COUNT, :]
+        unit = jnp.left_shift(jnp.ones_like(part), (part & 7) * 4)
+        for k in range(GROUPS // 8):
+            held = jnp.sum(jnp.where((part >> 3) == k, unit, 0), axis=0, keepdims=True)
+            nibble = jnp.broadcast_to(held, (8, 256)) >> (iota((8, 256), 0) * 4)
+            counts[parity, 8 * k : 8 * k + 8, :] = (nibble & 3).astype(f32)
+    second = [(counts[parity] == 2.0).astype(f32) for parity in range(2)]
+    both = (second[0] + second[1]).astype(bf16)
+    need_col = jnp.sum(second[0] + second[1], axis=1, keepdims=True)
+    need_row = lax.dot_general(
+        jnp.ones((8, 256), bf16), both, along_rows, preferred_element_type=f32
+    )[0:1, :]
+    g_col, g_row = iota((GROUPS, GROUPS), 0), iota((GROUPS, GROUPS), 1)
+    ahead = jnp.logical_or(
+        need_row > need_col, jnp.logical_and(need_row == need_col, g_row < g_col)
+    )
+    standing = jnp.sum(ahead.astype(i32), axis=1, keepdims=True)
+    position = (standing % ZS) * XS + standing // ZS
+    place[...] = jnp.broadcast_to(position, (GROUPS, 128))
+
+    cell = group * (PAIRS // 2) + pair // 2
+    line = dest_ref[pl.ds(cell, 1), :]
+    lane = iota((1, 128), 1)
+    mine = lane // COUNT == pair % 2
+    line = jnp.where(mine, line, -1)
+    eye = iota((128, 128), 0) == iota((128, 128), 1)
+    line_col = jnp.sum(jnp.where(eye, jnp.broadcast_to(line, (128, 128)), 0), axis=1, keepdims=True)
+    earlier = jnp.logical_and(line_col == line, iota((128, 128), 0) < iota((128, 128), 1))
+    rank = jnp.sum(earlier.astype(i32), axis=0, keepdims=True)
+    spot = jnp.sum(
+        jnp.where(iota((GROUPS, 128), 0) == line, place[...], 0), axis=0, keepdims=True
+    )
+    step = step_of((spot // XS - z + ZS) % ZS)
+    slot = jnp.where(rank == 0, step * XS + spot % XS, GROUPS + step)
+    slot = jnp.where(mine, slot, -1)
+    fold = slot[:, :COUNT] + slot[:, COUNT:] + 1
+    slot_col = jnp.sum(
+        jnp.where(
+            iota((COUNT, COUNT), 0) == iota((COUNT, COUNT), 1),
+            jnp.broadcast_to(fold, (COUNT, COUNT)),
+            0,
+        ),
+        axis=1,
+        keepdims=True,
+    )
+    pick[...] = (iota((SENT, COUNT), 0) == fold).astype(f32).astype(bf16)
+    unpick[...] = (iota((COUNT, SENT), 1) == slot_col).astype(f32).astype(bf16)
+    mark[...] = jnp.zeros((1, 128), i32)
+    mark[:, 0:PAIRS] = lab_ref[...]
+    marks[pl.ds(group, 1), :, :] = mark[...].reshape(1, 1, 128)
+
+    load_x.wait()
+
+    @pl.loop(0, COUNT // 16)
+    def _(i):
+        r = pl.ds(pl.multiple_of(i * 16, 16), 16)
+        values = xv[r, :].astype(f32)
+        factor = lax.rsqrt(jnp.mean(values * values, axis=-1, keepdims=True) + 1e-05)
+        hat[r, :] = (values * factor * (1.0 / math.sqrt(WIDTH))).astype(bf16)
+
+    @pl.loop(0, SUB, unroll=UNROLL)
+    def _(c):
+        got = jnp.dot(pick[...], hat[:, chunk(c)], preferred_element_type=f32)
+        spread(wide, c, 0, SENT, got)
+
+    send_s[...] = docs_of(wide, GROUPS, ZS)
+
+    def lab_x(j, source):
+        here = marks.at[pl.ds(z * XS + source, 1)]
+        return remote(here, here, lab_x_send.at[j], lab_x_recv.at[j], at(z, x_peer(j)))
+
+    def lab_z(t, plane, slot):
+        here = marks.at[pl.ds(plane * XS, XS)]
+        return remote(here, here, lab_z_send.at[t], lab_z_recv.at[slot], at(z_peer(t), x))
+
+    def r_out(t, j):
+        to = x_peer(j)
+        return remote(
+            send_r.at[t, to], own.at[0, mirror(t), x], r_send.at[t, j], r_recv.at[mirror(t), j],
+            at(z_peer(t), to),
+        )
+
+    def r_in(t, j):
+        source = lax.rem(x + XS - j, XS)
+        return remote(
+            send_r.at[t, source], own.at[0, t, source], r_send.at[t, j], r_recv.at[t, j],
+            at(z_peer(t), x_peer(j)),
+        )
+
+    def s_out(t, slot):
+        return remote(send_s.at[t], land_s.at[slot], s_send.at[t], s_recv.at[slot], at(z_peer(t), x))
+
+    def s_share(k, j, source):
+        four = pl.ds(k * QUAD, QUAD)
+        return remote(
+            land_s.at[four], own.at[1, four, source], m_send.at[k, j], m_recv.at[k, j],
+            at(z, x_peer(j)),
+        )
+
+    def yr_out(b, side):
+        two = pl.ds(b * BATCH, BATCH)
+        return remote(
+            own.at[0, two], beside.at[side, 0, two], yr_send.at[b, side], yr_recv.at[b, side],
+            (group, pair_peer(side)),
+        )
+
+    def ys_out(k, side):
+        four = pl.ds(k * QUAD, QUAD)
+        return remote(
+            own.at[1, four], beside.at[side, 1, four], ys_send.at[k, side], ys_recv.at[k, side],
+            (group, pair_peer(side)),
+        )
+
+    def r_batch(b, act):
+        for k in range(BATCH):
+            t = b * BATCH + k
+            for j in range(XS):
+                if j == 0 and k == 0:
+                    @pl.when(t > 0)
+                    def _():
+                        act(t, j)
+                else:
+                    act(t, j)
+
+    pl.semaphore_wait(barrier, GROUPS - 1 + 2)
+
+    for j in range(1, XS):
+        lab_x(j, x).start()
+
+    @pl.loop(1, ZS)
+    def _(t):
+        s_out(t, mirror(t)).start()
+
+    land_s[0] = send_s[0]
+
+    @pl.loop(0, BATCHES)
+    def _(b):
+        two = pl.ds(b * BATCH, BATCH)
+        send_r[two] = docs_of(wide, b * BATCH * XS, BATCH * XS).reshape(BATCH, XS, SUB, LANE)
+
+        @pl.when(b < AHEAD)
+        def _():
+            r_batch(b, lambda t, j: r_out(t, j).start())
+
+    own[0, 0, x] = send_r[0, x]
+
+    for j in range(1, XS):
+        lab_x(j, lax.rem(x + XS - j, XS)).wait_recv()
+
+    @pl.loop(1, ZS)
+    def _(t):
+        lab_z(t, z, mirror(t)).start()
+
+    @pl.loop(0, QUADS)
+    def _(k):
+        for i in range(QUAD):
+            t = k * QUAD + i
+            if i == 0:
+                @pl.when(t > 0)
+                def _():
+                    s_out(t, t).wait_recv()
+            else:
+                s_out(t, t).wait_recv()
+        for j in range(1, XS):
+            s_share(k, j, x).start()
+        for i in range(QUAD):
+            own[1, k * QUAD + i, x] = land_s[k * QUAD + i]
+
+    here = place[:, 0:1] == group
+    held = [
+        jnp.sum(jnp.where(here, counts[parity], 0.0), axis=0, keepdims=True) for parity in range(2)
+    ]
+    s_lane = iota((256, BLOCK), 1)
+    s_source = lax.rem(z + distance_at((s_lane // XS) % ZS), ZS) * XS + s_lane % XS
+    for n, shift in enumerate((0, PAIRS - 1, 1)):
+        other = lax.rem(pair + shift, PAIRS)
+        row = jnp.where(other % 2 == 0, held[0], held[1])
+        chosen = (iota((256, BLOCK), 0) == s_source * (PAIRS // 2) + other // 2).astype(f32)
+        filled = jnp.dot(
+            jnp.broadcast_to(row, (8, 256)).astype(bf16), chosen.astype(bf16),
+            preferred_element_type=f32,
+        )
+        lives[n] = (filled > (iota((8, BLOCK), 1) // GROUPS).astype(f32)).astype(f32)
+
+    at_here = (place[:, 0:GROUPS] == z * XS + iota((GROUPS, GROUPS), 1) % XS).astype(f32)
+    wanted = jnp.where(
+        pair % 2 == 0, (counts[0] == 2.0).astype(f32), (counts[1] == 2.0).astype(f32)
+    )
+    owner_of = lax.dot_general(
+        at_here.astype(bf16), wanted.astype(bf16), along_cols, preferred_element_type=f32
+    )
+    t_row = iota((GROUPS, 256), 0) // XS
+    c_row = (lax.rem(z + distance_at(t_row), ZS) * XS + x) * (PAIRS // 2) + pair // 2
+    choice[...] = jnp.broadcast_to(
+        jnp.sum(jnp.where(iota((GROUPS, 256), 1) == c_row, owner_of, 0.0), axis=1, keepdims=True),
+        (GROUPS, 128),
+    )
+
+    plane = (place[:, 0:ZS] // XS == iota((GROUPS, ZS), 1)).astype(f32).astype(bf16)
+    most = jnp.zeros((1, 1), f32)
+    for parity in range(2):
+        load = lax.dot_general(
+            plane, (counts[parity] == 2.0).astype(f32).astype(bf16), along_cols,
+            preferred_element_type=f32,
+        )
+        most = jnp.maximum(most, jnp.max(jnp.max(load, axis=1, keepdims=True), axis=0, keepdims=True))
+    ok_ref[...] = (most < 1.5).astype(i32)
+
+    def read_labels():
+        @pl.loop(1, ZS)
+        def _(t):
+            lab_z(t, z_peer(t), t).wait_recv()
+
+        def add_marks(g, total):
+            return total + jnp.where(place[pl.ds(g, 1), :] == group, marks[g], 0)
+
+        label = lax.fori_loop(0, GROUPS, add_marks, jnp.zeros((1, 128), i32))
+
+        def label_at(q):
+            return jnp.sum(jnp.where(lane == q, label, 0), axis=1, keepdims=True)
+
+        joined_prev = jnp.logical_and(label_at(pair - 1) == label_at(pair), pair > 0)
+        joined_next = jnp.logical_and(label_at(pair + 1) == label_at(pair), pair < PAIRS - 1)
+        sides[0] = jnp.broadcast_to(joined_prev.astype(f32), (8, 128))
+        sides[1] = jnp.broadcast_to(joined_next.astype(f32), (8, 128))
+
+    def to_rows(first):
+        @pl.loop(0, SUB, unroll=UNROLL)
+        def _(c):
+            rows[c, pl.ds(pl.multiple_of(first, 16), 16), :] = gather(wide, c, 16).astype(bf16)
+
+    def own_rows(kind, k):
+        put_wide(wide, 0, own[kind, pl.ds(k * QUAD, QUAD)].reshape(16, SUB, LANE))
+        to_rows(kind * GROUPS + k * 16)
+
+    def beside_rows(kind, k):
+        four = pl.ds(k * QUAD, QUAD)
+        flag = sides[0][0:1, :]
+        flag = jnp.broadcast_to(jnp.concatenate([flag, flag], axis=1), (16 * SUB, LANE))
+        prev = beside[0, kind, four].reshape(16 * SUB, LANE).astype(f32)
+        nxt = beside[1, kind, four].reshape(16 * SUB, LANE).astype(f32)
+        put_wide(wide, 0, jnp.where(flag > 0.5, prev, nxt).reshape(16, SUB, LANE))
+        to_rows(BLOCK + kind * GROUPS + k * 16)
+
+    @pl.loop(0, QUADS)
+    def _(k):
+        for j in range(1, XS):
+            s_share(k, j, lax.rem(x + XS - j, XS)).wait_recv()
+        for side in range(2):
+            ys_out(k, side).start()
+
+    @pl.loop(0, BATCHES)
+    def _(b):
+        r_batch(b, lambda t, j: r_in(t, j).wait_recv())
+
+        @pl.when(b + AHEAD < BATCHES)
+        def _():
+            r_batch(b + AHEAD, lambda t, j: r_out(t, j).start())
+
+        for side in range(2):
+            yr_out(b, side).start()
+
+        @pl.when(b % 2 == 1)
+        def _():
+            own_rows(0, b // 2)
+            own_rows(1, b // 2)
+
+        pl.when(b == 3)(read_labels)
+
+        @pl.when(b >= 4)
+        def _():
+            k = b - 4
+            for side in range(2):
+                ys_out(k, side).wait_recv()
+            beside_rows(1, k)
+
+    def add_own(c, total):
+        mine = rows[c, 0:BLOCK]
+        return total + lax.dot_general(mine, mine, along_rows, preferred_element_type=f32)
+
+    scores[:, 0:BLOCK] = lax.fori_loop(
+        0, SUB, add_own, jnp.zeros((BLOCK, BLOCK), f32), unroll=UNROLL
+    )
+
+    @pl.loop(0, QUADS)
+    def _(k):
+        for i in range(2):
+            for side in range(2):
+                yr_out(2 * k + i, side).wait_recv()
+        beside_rows(0, k)
+
+    prev_mask = lives[1][0:1, :] * sides[0][0:1, :]
+    next_mask = lives[2][0:1, :] * sides[1][0:1, :]
+    side_mask = jnp.broadcast_to(prev_mask + next_mask, (GROUPS, BLOCK))
+
+    def smooth(kind):
+        part = pl.ds(kind * GROUPS, GROUPS)
+
+        def add_side(c, total):
+            return total + lax.dot_general(
+                rows[c, part], rows[c, BLOCK : 2 * BLOCK], along_rows, preferred_element_type=f32
+            )
+
+        scores[part, BLOCK : 2 * BLOCK] = lax.fori_loop(
+            0, SUB, add_side, jnp.zeros((GROUPS, BLOCK), f32), unroll=UNROLL
+        )
+        apart = (iota((GROUPS, BLOCK), 0) + kind * GROUPS != iota((GROUPS, BLOCK), 1)).astype(f32)
+        mask = jnp.concatenate([lives[0][0:1, :] * apart, side_mask], axis=1)
+        raw = jnp.exp(score_scale * scores[part, :]) * mask
+        weights[...] = raw.astype(bf16)
+        denom = self_weight + jnp.sum(raw, axis=1, keepdims=True)
+        scale = jnp.broadcast_to(math.sqrt(WIDTH) / denom, (GROUPS, LANE))
+
+        @pl.loop(0, SUB, unroll=UNROLL)
+        def _(c):
+            numer = self_weight * rows[c, part].astype(f32) + jnp.dot(
+                weights[...], rows[c], preferred_element_type=f32
+            )
+            spread(wide, c, kind * GROUPS, GROUPS, numer * scale)
+
+    def r_home(t, j):
+        to = x_peer(j)
+        return remote(
+            out_r.at[t, to], ret_r.at[mirror(t), x], rb_send.at[t, j], rb_recv.at[mirror(t), j],
+            at(z_peer(t), to),
+        )
+
+    def r_arrival(t, j):
+        source = lax.rem(x + XS - j, XS)
+        return remote(
+            out_r.at[t, source], ret_r.at[t, source], rb_send.at[t, j], rb_recv.at[t, j],
+            at(z_peer(t), x_peer(j)),
+        )
+
+    def s_back(k, j, to, target):
+        four = pl.ds(k * QUAD, QUAD)
+        return remote(
+            out_s.at[four, to], cand.at[four, target], mb_send.at[k, j], mb_recv.at[k, j],
+            at(z, x_peer(j)),
+        )
+
+    def s_home(t, slot):
+        return remote(back_s.at[t], ret_s.at[slot], sb_send.at[t], sb_recv.at[slot], at(z_peer(t), x))
+
+    smooth(0)
+
+    @pl.loop(0, BATCHES)
+    def _(b):
+        two = pl.ds(b * BATCH, BATCH)
+        out_r[two] = docs_of(wide, b * BATCH * XS, BATCH * XS).reshape(BATCH, XS, SUB, LANE)
+        r_batch(b, lambda t, j: r_home(t, j).start())
+
+    ret_r[0, x] = out_r[0, x]
+
+    smooth(1)
+
+    @pl.loop(0, QUADS)
+    def _(k):
+        four = pl.ds(k * QUAD, QUAD)
+        out_s[four] = docs_of(wide, GROUPS + k * 16, 16).reshape(QUAD, XS, SUB, LANE)
+        for j in range(1, XS):
+            s_back(k, j, x_peer(j), x).start()
+        for i in range(QUAD):
+            cand[k * QUAD + i, x] = out_s[k * QUAD + i, x]
+
+    def choose(t):
+        chosen = cand[t, XS - 1].astype(f32)
+        for k in range(XS - 1):
+            flag = choice[pl.ds(t * XS + k, 1), :]
+            flag = jnp.broadcast_to(jnp.concatenate([flag, flag], axis=1), (SUB, LANE))
+            chosen = jnp.where(flag > 0.5, cand[t, k].astype(f32), chosen)
+        back_s[t] = chosen.astype(bf16)
+
+    @pl.loop(0, QUADS)
+    def _(k):
+        for j in range(1, XS):
+            s_back(k, j, x, lax.rem(x + XS - j, XS)).wait_recv()
+        for i in range(QUAD):
+            t = k * QUAD + i
+            choose(t)
+            if i == 0:
+                @pl.when(t > 0)
+                def _():
+                    s_home(t, mirror(t)).start()
+            else:
+                s_home(t, mirror(t)).start()
+
+    ret_s[0] = back_s[0]
+
+    @pl.loop(0, BATCHES)
+    def _(b):
+        r_batch(b, lambda t, j: r_arrival(t, j).wait_recv())
+        two = pl.ds(b * BATCH, BATCH)
+        put_wide(wide, b * BATCH * XS, ret_r[two].reshape(BATCH * XS, SUB, LANE))
+
+    @pl.loop(1, ZS)
+    def _(t):
+        s_home(t, t).wait_recv()
+
+    put_wide(wide, GROUPS, ret_s[...])
+
+    @pl.loop(0, SUB, unroll=UNROLL)
+    def _(c):
+        got = gather(wide, c, SENT).astype(bf16)
+        out_ref[:, chunk(c)] = jnp.dot(unpick[...], got, preferred_element_type=f32).astype(bf16)
+
+    for j in range(1, XS):
+        lab_x(j, x).wait_send()
+
+    @pl.loop(1, ZS)
+    def _(t):
+        lab_z(t, z, mirror(t)).wait_send()
+        s_out(t, mirror(t)).wait_send()
+        s_home(t, mirror(t)).wait_send()
+
+    @pl.loop(0, BATCHES)
+    def _(b):
+        r_batch(b, lambda t, j: r_out(t, j).wait_send())
+        r_batch(b, lambda t, j: r_home(t, j).wait_send())
+        for side in range(2):
+            yr_out(b, side).wait_send()
+
+    @pl.loop(0, QUADS)
+    def _(k):
+        for j in range(1, XS):
+            s_share(k, j, x).wait_send()
+            s_back(k, j, x_peer(j), x).wait_send()
+        for side in range(2):
+            ys_out(k, side).wait_send()
+
+
+def compact(embeddings, dest, labels):
+    vmem = pl.BlockSpec(memory_space=pltpu.VMEM)
+    dma = pltpu.SemaphoreType.DMA
+    return pl.pallas_call(
+        compact_kernel,
+        out_shape=(
+            jax.ShapeDtypeStruct((COUNT, WIDTH), bf16),
+            jax.ShapeDtypeStruct((1, 1), i32),
+        ),
+        in_specs=[pl.BlockSpec(memory_space=pl.ANY), vmem, vmem],
+        out_specs=(vmem, vmem),
+        scratch_shapes=[
+            pltpu.VMEM((COUNT, WIDTH), bf16),
+            pltpu.VMEM((COUNT, WIDTH), bf16),
+            pltpu.VMEM((2, BLOCK * SUB, 128), f32),
+            pltpu.VMEM((ZS, XS, SUB, LANE), bf16),
+            pltpu.VMEM((ZS, SUB, LANE), bf16),
+            pltpu.VMEM((ZS, SUB, LANE), bf16),
+            pltpu.VMEM((2, ZS, XS, SUB, LANE), bf16),
+            pltpu.VMEM((2, 2, ZS, XS, SUB, LANE), bf16),
+            pltpu.VMEM((SUB, 2 * BLOCK, LANE), bf16),
+            pltpu.VMEM((ZS, XS, SUB, LANE), bf16),
+            pltpu.VMEM((ZS, XS, SUB, LANE), bf16),
+            pltpu.VMEM((ZS, SUB, LANE), bf16),
+            pltpu.VMEM((ZS, XS, SUB, LANE), bf16),
+            pltpu.VMEM((ZS, XS, SUB, LANE), bf16),
+            pltpu.VMEM((ZS, SUB, LANE), bf16),
+            pltpu.VMEM((1, 128), i32),
+            pltpu.VMEM((GROUPS, 1, 128), i32),
+            pltpu.VMEM((2, GROUPS, 256), f32),
+            pltpu.VMEM((GROUPS, 128), i32),
+            pltpu.VMEM((SENT, COUNT), bf16),
+            pltpu.VMEM((COUNT, SENT), bf16),
+            pltpu.VMEM((2, 8, 128), f32),
+            pltpu.VMEM((3, 8, BLOCK), f32),
+            pltpu.VMEM((GROUPS, 128), f32),
+            pltpu.VMEM((GROUPS, 2 * BLOCK), bf16),
+            pltpu.VMEM((BLOCK, 2 * BLOCK), f32),
+            dma(()),
+            dma((XS,)), dma((XS,)), dma((ZS,)), dma((ZS,)),
+            dma((ZS, XS)), dma((ZS, XS)), dma((ZS,)), dma((ZS,)), dma((QUADS, XS)), dma((QUADS, XS)),
+            dma((BATCHES, 2)), dma((BATCHES, 2)), dma((QUADS, 2)), dma((QUADS, 2)),
+            dma((ZS, XS)), dma((ZS, XS)), dma((QUADS, XS)), dma((QUADS, XS)), dma((ZS,)), dma((ZS,)),
+        ],
+        compiler_params=pltpu.CompilerParams(
+            collective_id=0, has_side_effects=True, vmem_limit_bytes=40 << 20
+        ),
+    )(embeddings, dest, labels)
+
+
+def on_device(embeddings, dest, labels):
+    out, ok = compact(embeddings, dest.reshape(GROUPS * PAIRS * COUNT // 128, 128), labels)
+    return lax.cond(ok.reshape(()) == 1, lambda: out, lambda: padded(embeddings, dest, labels))
+
+
 def solution(mesh):
     in_specs = (P(("group", "pair"), None), P(), P("group", None))
     out_specs = P(("group", "pair"), None)

time: 179 us -> 99.6 us (0.56)
  the two profiles are of different devices: /device:TPU:10 before, /device:TPU:1 now
where the time goes in v2:
time: 99.6 us; the launch traced here: 99.4 us
  Pallas kernels  97.7 us (98%)
    pallas_call x1, Pallas kernels, compact(): pl.pallas_call(compact_kernel, out_shape=(jax.ShapeDtypeStruct((COUNT, WI...  97.7 us

profile of v2, /device:TPU:1, one launch (start us, length us, event | category | flops | bytes accessed | tf_op | source)
XLA Modules:
  0.0 99.4 jit_solution(6080448945390933091)
XLA Ops:
  0.0 97.7 %shard_map.39 = (bf16[64,4096]{1,0:T(8,128)(2,1)S(1)}, s32[1,1]{1,0:T(1,128)}) custom-call(bf16[64,4096]{1,0:T(8,128)(2,1)} %x_ref.1, s32[256,128]{1,0:T(8,128)} %bitcast.29, s32[1,8]{1,0:T(1,128)} %lab_ref.1), custom_call_target="tpu_custom_call" | custom-call | tf_op jit(solution)/shard_map/pallas_call | solution.py:648
  98.4 0.2 conditional.1
  98.6 0.8 copy.13

commit v3 on v2

--- a/solution.py
+++ b/solution.py
@@ -113,8 +113,9 @@
 BATCHES = ZS // BATCH
 QUAD = 4
 QUADS = ZS // QUAD
-AHEAD = 3
-UNROLL = 4
+AHEAD = 5
+UNROLL = 8
+FIRST = 4
 MESH = pl.DeviceIdType.MESH
 f32, bf16, i32 = jnp.float32, jnp.bfloat16, jnp.int32
 
@@ -165,10 +166,10 @@
 
 
 def compact_kernel(
-    x_ref, dest_ref, lab_ref, out_ref, ok_ref,
-    xv, hat, wide, send_r, send_s, land_s, own, beside, rows, out_r, out_s, back_s, cand, ret_r, ret_s,
+    x_ref, dest_hbm, lab_ref, out_ref, ok_ref,
+    dest_ref, xv, hat, wide, send_r, send_s, land_s, own, beside, rows, out_r, out_s, back_s, cand, ret_r, ret_s,
     mark, marks, counts, place, pick, unpick, sides, lives, choice, weights, scores,
-    in_sem, lab_x_send, lab_x_recv, lab_z_send, lab_z_recv,
+    in_sem, lab_send, lab_recv,
     r_send, r_recv, s_send, s_recv, m_send, m_recv, yr_send, yr_recv, ys_send, ys_recv,
     rb_send, rb_recv, mb_send, mb_recv, sb_send, sb_recv,
 ):
@@ -193,6 +194,10 @@
             source, target, send, recv, device_id=device, device_id_type=MESH
         )
 
+    load_x = pltpu.make_async_copy(x_ref, xv, in_sem.at[0])
+    load_dest = pltpu.make_async_copy(dest_hbm, dest_ref, in_sem.at[1])
+    load_dest.start()
+    load_x.start()
     barrier = pltpu.get_barrier_semaphore()
 
     @pl.loop(1, GROUPS)
@@ -206,9 +211,7 @@
             barrier, inc=1, device_id=(group, lax.rem(pair + step, PAIRS)), device_id_type=MESH
         )
 
-    load_x = pltpu.make_async_copy(x_ref, xv, in_sem)
-    load_x.start()
-
+    load_dest.wait()
     turned = dest_ref[...].T
     for parity in range(2):
         part = turned[parity * COUNT : (parity + 1) * COUNT, :]
@@ -278,49 +281,39 @@
 
     send_s[...] = docs_of(wide, GROUPS, ZS)
 
-    def lab_x(j, source):
-        here = marks.at[pl.ds(z * XS + source, 1)]
-        return remote(here, here, lab_x_send.at[j], lab_x_recv.at[j], at(z, x_peer(j)))
-
-    def lab_z(t, plane, slot):
-        here = marks.at[pl.ds(plane * XS, XS)]
-        return remote(here, here, lab_z_send.at[t], lab_z_recv.at[slot], at(z_peer(t), x))
+    def lab_x(j):
+        here = marks.at[pl.ds(group, 1)]
+        return remote(here, here, lab_send.at[0], lab_recv.at[0], at(z, x_peer(j)))
+
+    def lab_z(t):
+        here = marks.at[pl.ds(z * XS, XS)]
+        return remote(here, here, lab_send.at[1], lab_recv.at[1], at(z_peer(t), x))
 
     def r_out(t, j):
         to = x_peer(j)
         return remote(
-            send_r.at[t, to], own.at[0, mirror(t), x], r_send.at[t, j], r_recv.at[mirror(t), j],
+            send_r.at[t * XS + to], own.at[0, mirror(t), x], r_send, r_recv.at[t // BATCH],
             at(z_peer(t), to),
         )
 
-    def r_in(t, j):
-        source = lax.rem(x + XS - j, XS)
-        return remote(
-            send_r.at[t, source], own.at[0, t, source], r_send.at[t, j], r_recv.at[t, j],
-            at(z_peer(t), x_peer(j)),
-        )
-
-    def s_out(t, slot):
-        return remote(send_s.at[t], land_s.at[slot], s_send.at[t], s_recv.at[slot], at(z_peer(t), x))
-
-    def s_share(k, j, source):
+    def s_out(t):
+        return remote(send_s.at[t], land_s.at[mirror(t)], s_send, s_recv.at[t // QUAD], at(z_peer(t), x))
+
+    def s_share(k, j):
         four = pl.ds(k * QUAD, QUAD)
-        return remote(
-            land_s.at[four], own.at[1, four, source], m_send.at[k, j], m_recv.at[k, j],
-            at(z, x_peer(j)),
-        )
+        return remote(land_s.at[four], own.at[1, four, x], m_send, m_recv.at[k], at(z, x_peer(j)))
 
     def yr_out(b, side):
         two = pl.ds(b * BATCH, BATCH)
         return remote(
-            own.at[0, two], beside.at[side, 0, two], yr_send.at[b, side], yr_recv.at[b, side],
+            own.at[0, two], beside.at[side, 0, two], yr_send, yr_recv.at[b],
             (group, pair_peer(side)),
         )
 
     def ys_out(k, side):
         four = pl.ds(k * QUAD, QUAD)
         return remote(
-            own.at[1, four], beside.at[side, 1, four], ys_send.at[k, side], ys_recv.at[k, side],
+            own.at[1, four], beside.at[side, 1, four], ys_send, ys_recv.at[k],
             (group, pair_peer(side)),
         )
 
@@ -335,49 +328,45 @@
                 else:
                     act(t, j)
 
+    def local(source, target, sem):
+        pltpu.make_async_copy(source, target, sem).start()
+
+    def settle(arrived, sem):
+        pltpu.make_async_copy(arrived, arrived, sem).wait()
+
     pl.semaphore_wait(barrier, GROUPS - 1 + 2)
 
     for j in range(1, XS):
-        lab_x(j, x).start()
+        lab_x(j).start()
 
     @pl.loop(1, ZS)
     def _(t):
-        s_out(t, mirror(t)).start()
-
-    land_s[0] = send_s[0]
+        s_out(t).start()
+
+    local(send_s.at[0], land_s.at[0], s_recv.at[0])
 
     @pl.loop(0, BATCHES)
     def _(b):
-        two = pl.ds(b * BATCH, BATCH)
-        send_r[two] = docs_of(wide, b * BATCH * XS, BATCH * XS).reshape(BATCH, XS, SUB, LANE)
+        send_r[pl.ds(b * BATCH * XS, BATCH * XS)] = docs_of(wide, b * BATCH * XS, BATCH * XS)
 
         @pl.when(b < AHEAD)
         def _():
             r_batch(b, lambda t, j: r_out(t, j).start())
 
-    own[0, 0, x] = send_r[0, x]
-
-    for j in range(1, XS):
-        lab_x(j, lax.rem(x + XS - j, XS)).wait_recv()
+    local(send_r.at[x], own.at[0, 0, x], r_recv.at[0])
+    settle(marks.at[pl.ds(0, XS - 1)], lab_recv.at[0])
 
     @pl.loop(1, ZS)
     def _(t):
-        lab_z(t, z, mirror(t)).start()
+        lab_z(t).start()
 
     @pl.loop(0, QUADS)
     def _(k):
-        for i in range(QUAD):
-            t = k * QUAD + i
-            if i == 0:
-                @pl.when(t > 0)
-                def _():
-                    s_out(t, t).wait_recv()
-            else:
-                s_out(t, t).wait_recv()
+        four = pl.ds(k * QUAD, QUAD)
+        settle(land_s.at[four], s_recv.at[k])
         for j in range(1, XS):
-            s_share(k, j, x).start()
-        for i in range(QUAD):
-            own[1, k * QUAD + i, x] = land_s[k * QUAD + i]
+            s_share(k, j).start()
+        local(land_s.at[four], own.at[1, four, x], m_recv.at[k])
 
     here = place[:, 0:1] == group
     held = [
@@ -420,9 +409,7 @@
     ok_ref[...] = (most < 1.5).astype(i32)
 
     def read_labels():
-        @pl.loop(1, ZS)
-        def _(t):
-            lab_z(t, z_peer(t), t).wait_recv()
+        settle(marks.at[pl.ds(0, GROUPS - XS)], lab_recv.at[1])
 
         def add_marks(g, total):
             return total + jnp.where(place[pl.ds(g, 1), :] == group, marks[g], 0)
@@ -455,16 +442,21 @@
         put_wide(wide, 0, jnp.where(flag > 0.5, prev, nxt).reshape(16, SUB, LANE))
         to_rows(BLOCK + kind * GROUPS + k * 16)
 
+    def beside_r(k):
+        for i in range(2):
+            two = pl.ds((2 * k + i) * BATCH, BATCH)
+            settle(beside.at[:, 0, two], yr_recv.at[2 * k + i])
+        beside_rows(0, k)
+
     @pl.loop(0, QUADS)
     def _(k):
-        for j in range(1, XS):
-            s_share(k, j, lax.rem(x + XS - j, XS)).wait_recv()
+        settle(own.at[1, pl.ds(k * QUAD, QUAD)], m_recv.at[k])
         for side in range(2):
             ys_out(k, side).start()
 
     @pl.loop(0, BATCHES)
     def _(b):
-        r_batch(b, lambda t, j: r_in(t, j).wait_recv())
+        settle(own.at[0, pl.ds(b * BATCH, BATCH)], r_recv.at[b])
 
         @pl.when(b + AHEAD < BATCHES)
         def _():
@@ -483,9 +475,12 @@
         @pl.when(b >= 4)
         def _():
             k = b - 4
-            for side in range(2):
-                ys_out(k, side).wait_recv()
+            settle(beside.at[:, 1, pl.ds(k * QUAD, QUAD)], ys_recv.at[k])
             beside_rows(1, k)
+
+            @pl.when(k >= 2)
+            def _():
+                beside_r(k - 2)
 
     def add_own(c, total):
         mine = rows[c, 0:BLOCK]
@@ -495,12 +490,9 @@
         0, SUB, add_own, jnp.zeros((BLOCK, BLOCK), f32), unroll=UNROLL
     )
 
-    @pl.loop(0, QUADS)
+    @pl.loop(2, QUADS)
     def _(k):
-        for i in range(2):
-            for side in range(2):
-                yr_out(2 * k + i, side).wait_recv()
-        beside_rows(0, k)
+        beside_r(k)
 
     prev_mask = lives[1][0:1, :] * sides[0][0:1, :]
     next_mask = lives[2][0:1, :] * sides[1][0:1, :]
@@ -534,36 +526,28 @@
     def r_home(t, j):
         to = x_peer(j)
         return remote(
-            out_r.at[t, to], ret_r.at[mirror(t), x], rb_send.at[t, j], rb_recv.at[mirror(t), j],
+            out_r.at[t * XS + to], ret_r.at[mirror(t), x], rb_send, rb_recv.at[t // BATCH],
             at(z_peer(t), to),
         )
 
-    def r_arrival(t, j):
-        source = lax.rem(x + XS - j, XS)
-        return remote(
-            out_r.at[t, source], ret_r.at[t, source], rb_send.at[t, j], rb_recv.at[t, j],
-            at(z_peer(t), x_peer(j)),
-        )
-
-    def s_back(k, j, to, target):
-        four = pl.ds(k * QUAD, QUAD)
-        return remote(
-            out_s.at[four, to], cand.at[four, target], mb_send.at[k, j], mb_recv.at[k, j],
-            at(z, x_peer(j)),
-        )
-
-    def s_home(t, slot):
-        return remote(back_s.at[t], ret_s.at[slot], sb_send.at[t], sb_recv.at[slot], at(z_peer(t), x))
+    def s_back(k, j):
+        four, to = pl.ds(k * QUAD, QUAD), x_peer(j)
+        return remote(out_s.at[four, to], cand.at[four, x], mb_send, mb_recv.at[k], at(z, to))
+
+    def s_home(t):
+        return remote(back_s.at[t], ret_s.at[mirror(t)], sb_send, sb_recv, at(z_peer(t), x))
 
     smooth(0)
 
     @pl.loop(0, BATCHES)
     def _(b):
-        two = pl.ds(b * BATCH, BATCH)
-        out_r[two] = docs_of(wide, b * BATCH * XS, BATCH * XS).reshape(BATCH, XS, SUB, LANE)
-        r_batch(b, lambda t, j: r_home(t, j).start())
-
-    ret_r[0, x] = out_r[0, x]
+        out_r[pl.ds(b * BATCH * XS, BATCH * XS)] = docs_of(wide, b * BATCH * XS, BATCH * XS)
+
+        @pl.when(b < FIRST)
+        def _():
+            r_batch(b, lambda t, j: r_home(t, j).start())
+
+    local(out_r.at[x], ret_r.at[0, x], rb_recv.at[0])
 
     smooth(1)
 
@@ -572,9 +556,8 @@
         four = pl.ds(k * QUAD, QUAD)
         out_s[four] = docs_of(wide, GROUPS + k * 16, 16).reshape(QUAD, XS, SUB, LANE)
         for j in range(1, XS):
-            s_back(k, j, x_peer(j), x).start()
-        for i in range(QUAD):
-            cand[k * QUAD + i, x] = out_s[k * QUAD + i, x]
+            s_back(k, j).start()
+        local(out_s.at[four, x], cand.at[four, x], mb_recv.at[k])
 
     def choose(t):
         chosen = cand[t, XS - 1].astype(f32)
@@ -586,30 +569,30 @@
 
     @pl.loop(0, QUADS)
     def _(k):
-        for j in range(1, XS):
-            s_back(k, j, x, lax.rem(x + XS - j, XS)).wait_recv()
+        settle(cand.at[pl.ds(k * QUAD, QUAD)], mb_recv.at[k])
         for i in range(QUAD):
             t = k * QUAD + i
             choose(t)
             if i == 0:
                 @pl.when(t > 0)
                 def _():
-                    s_home(t, mirror(t)).start()
+                    s_home(t).start()
             else:
-                s_home(t, mirror(t)).start()
-
-    ret_s[0] = back_s[0]
+                s_home(t).start()
+
+    @pl.loop(FIRST, BATCHES)
+    def _(b):
+        r_batch(b, lambda t, j: r_home(t, j).start())
+
+    local(back_s.at[0], ret_s.at[0], sb_recv)
 
     @pl.loop(0, BATCHES)
     def _(b):
-        r_batch(b, lambda t, j: r_arrival(t, j).wait_recv())
         two = pl.ds(b * BATCH, BATCH)
+        settle(ret_r.at[two], rb_recv.at[b])
         put_wide(wide, b * BATCH * XS, ret_r[two].reshape(BATCH * XS, SUB, LANE))
 
-    @pl.loop(1, ZS)
-    def _(t):
-        s_home(t, t).wait_recv()
-
+    settle(ret_s, sb_recv)
     put_wide(wide, GROUPS, ret_s[...])
 
     @pl.loop(0, SUB, unroll=UNROLL)
@@ -617,29 +600,16 @@
         got = gather(wide, c, SENT).astype(bf16)
         out_ref[:, chunk(c)] = jnp.dot(unpick[...], got, preferred_element_type=f32).astype(bf16)
 
-    for j in range(1, XS):
-        lab_x(j, x).wait_send()
-
-    @pl.loop(1, ZS)
-    def _(t):
-        lab_z(t, z, mirror(t)).wait_send()
-        s_out(t, mirror(t)).wait_send()
-        s_home(t, mirror(t)).wait_send()
-
-    @pl.loop(0, BATCHES)
-    def _(b):
-        r_batch(b, lambda t, j: r_out(t, j).wait_send())
-        r_batch(b, lambda t, j: r_home(t, j).wait_send())
-        for side in range(2):
-            yr_out(b, side).wait_send()
-
-    @pl.loop(0, QUADS)
-    def _(k):
-        for j in range(1, XS):
-            s_share(k, j, x).wait_send()
-            s_back(k, j, x_peer(j), x).wait_send()
-        for side in range(2):
-            ys_out(k, side).wait_send()
+    settle(marks.at[pl.ds(0, XS - 1)], lab_send.at[0])
+    settle(marks.at[pl.ds(0, GROUPS - XS)], lab_send.at[1])
+    settle(send_r.at[pl.ds(0, GROUPS - 1)], r_send)
+    settle(send_s.at[pl.ds(0, ZS - 1)], s_send)
+    settle(send_r.at[pl.ds(0, GROUPS - ZS)], m_send)
+    settle(own, yr_send)
+    settle(own, ys_send)
+    settle(out_r.at[pl.ds(0, GROUPS - 1)], rb_send)
+    settle(out_r.at[pl.ds(0, GROUPS - ZS)], mb_send)
+    settle(back_s.at[pl.ds(0, ZS - 1)], sb_send)
 
 
 def compact(embeddings, dest, labels):
@@ -651,19 +621,20 @@
             jax.ShapeDtypeStruct((COUNT, WIDTH), bf16),
             jax.ShapeDtypeStruct((1, 1), i32),
         ),
-        in_specs=[pl.BlockSpec(memory_space=pl.ANY), vmem, vmem],
+        in_specs=[pl.BlockSpec(memory_space=pl.ANY)] * 2 + [vmem],
         out_specs=(vmem, vmem),
         scratch_shapes=[
+            pltpu.VMEM((256, 128), i32),
             pltpu.VMEM((COUNT, WIDTH), bf16),
             pltpu.VMEM((COUNT, WIDTH), bf16),
             pltpu.VMEM((2, BLOCK * SUB, 128), f32),
-            pltpu.VMEM((ZS, XS, SUB, LANE), bf16),
+            pltpu.VMEM((GROUPS, SUB, LANE), bf16),
             pltpu.VMEM((ZS, SUB, LANE), bf16),
             pltpu.VMEM((ZS, SUB, LANE), bf16),
             pltpu.VMEM((2, ZS, XS, SUB, LANE), bf16),
             pltpu.VMEM((2, 2, ZS, XS, SUB, LANE), bf16),
             pltpu.VMEM((SUB, 2 * BLOCK, LANE), bf16),
-            pltpu.VMEM((ZS, XS, SUB, LANE), bf16),
+            pltpu.VMEM((GROUPS, SUB, LANE), bf16),
             pltpu.VMEM((ZS, XS, SUB, LANE), bf16),
             pltpu.VMEM((ZS, SUB, LANE), bf16),
             pltpu.VMEM((ZS, XS, SUB, LANE), bf16),
@@ -680,11 +651,10 @@
             pltpu.VMEM((GROUPS, 128), f32),
             pltpu.VMEM((GROUPS, 2 * BLOCK), bf16),
             pltpu.VMEM((BLOCK, 2 * BLOCK), f32),
-            dma(()),
-            dma((XS,)), dma((XS,)), dma((ZS,)), dma((ZS,)),
-            dma((ZS, XS)), dma((ZS, XS)), dma((ZS,)), dma((ZS,)), dma((QUADS, XS)), dma((QUADS, XS)),
-            dma((BATCHES, 2)), dma((BATCHES, 2)), dma((QUADS, 2)), dma((QUADS, 2)),
-            dma((ZS, XS)), dma((ZS, XS)), dma((QUADS, XS)), dma((QUADS, XS)), dma((ZS,)), dma((ZS,)),
+            dma((2,)), dma((2,)), dma((2,)),
+            dma(()), dma((BATCHES,)), dma(()), dma((QUADS,)), dma(()), dma((QUADS,)),
+            dma(()), dma((BATCHES,)), dma(()), dma((QUADS,)),
+            dma(()), dma((BATCHES,)), dma(()), dma((QUADS,)), dma(()), dma(()),
         ],
         compiler_params=pltpu.CompilerParams(
             collective_id=0, has_side_effects=True, vmem_limit_bytes=40 << 20

time: 99.6 us -> 91.4 us (0.918)
  Pallas kernels: 97.7 us -> 89.5 us
    pallas_call x1, Pallas kernels: 97.7 us -> 89.5 us  [compact(): pl.pallas_call(compact_kernel, out_shape=(jax.ShapeDtypeStruct((COUNT, WI...]
where the time goes in v3:
time: 91.4 us; the launch traced here: 91.3 us
  Pallas kernels  89.5 us (98%)
    pallas_call x1, Pallas kernels, compact(): pl.pallas_call(compact_kernel, out_shape=(jax.ShapeDtypeStruct((COUNT, WI...  89.5 us

profile of v3, /device:TPU:1, one launch (start us, length us, event | category | flops | bytes accessed | tf_op | source)
XLA Modules:
  0.0 91.3 jit_solution(14220463176611125150)
XLA Ops:
  0.0 89.5 %shard_map.39 = (bf16[64,4096]{1,0:T(8,128)(2,1)S(1)}, s32[1,1]{1,0:T(1,128)}) custom-call(bf16[64,4096]{1,0:T(8,128)(2,1)} %x_ref.1, s32[256,128]{1,0:T(8,128)} %bitcast.29, s32[1,8]{1,0:T(1,128)} %lab_ref.1), custom_call_target="tpu_custom_call" | custom-call | tf_op jit(solution)/shard_map/pallas_call | solution.py:618
  90.2 0.2 conditional.1
  90.5 0.8 copy.13

commit v4 on v3

--- a/solution.py
+++ b/solution.py
@@ -114,7 +114,7 @@
 QUAD = 4
 QUADS = ZS // QUAD
 AHEAD = 5
-UNROLL = 8
+UNROLL = 16
 FIRST = 4
 MESH = pl.DeviceIdType.MESH
 f32, bf16, i32 = jnp.float32, jnp.bfloat16, jnp.int32

time: 91.4 us -> 91 us (level)
  no operation moved by 1% of the time
where the time goes in v4:
time: 91 us; the launch traced here: 90.9 us
  Pallas kernels  89.1 us (98%)
    pallas_call x1, Pallas kernels, compact(): pl.pallas_call(compact_kernel, out_shape=(jax.ShapeDtypeStruct((COUNT, WI...  89.1 us

profile of v4, /device:TPU:1, one launch (start us, length us, event | category | flops | bytes accessed | tf_op | source)
XLA Modules:
  0.0 90.9 jit_solution(5123193641479344287)
XLA Ops:
  0.0 89.1 %shard_map.39 = (bf16[64,4096]{1,0:T(8,128)(2,1)S(1)}, s32[1,1]{1,0:T(1,128)}) custom-call(bf16[64,4096]{1,0:T(8,128)(2,1)} %x_ref.1, s32[256,128]{1,0:T(8,128)} %bitcast.29, s32[1,8]{1,0:T(1,128)} %lab_ref.1), custom_call_target="tpu_custom_call" | custom-call | tf_op jit(solution)/shard_map/pallas_call | solution.py:618
  89.8 0.2 conditional.1
  90.1 0.8 copy.13

commit v5 on v4

--- a/solution.py
+++ b/solution.py
@@ -627,7 +627,7 @@
             pltpu.VMEM((256, 128), i32),
             pltpu.VMEM((COUNT, WIDTH), bf16),
             pltpu.VMEM((COUNT, WIDTH), bf16),
-            pltpu.VMEM((2, BLOCK * SUB, 128), f32),
+            pltpu.VMEM((2, (BLOCK + 1) * SUB, 128), f32),
             pltpu.VMEM((GROUPS, SUB, LANE), bf16),
             pltpu.VMEM((ZS, SUB, LANE), bf16),
             pltpu.VMEM((ZS, SUB, LANE), bf16),

time: 91 us -> 91 us (level)
  no operation moved by 1% of the time
where the time goes in v5:
time: 91 us; the launch traced here: 90.9 us
  Pallas kernels  89.1 us (98%)
    pallas_call x1, Pallas kernels, compact(): pl.pallas_call(compact_kernel, out_shape=(jax.ShapeDtypeStruct((COUNT, WI...  89.1 us

profile of v5, /device:TPU:1, one launch (start us, length us, event | category | flops | bytes accessed | tf_op | source)
XLA Modules:
  0.0 90.9 jit_solution(17099648100691205391)
XLA Ops:
  0.0 89.1 %shard_map.39 = (bf16[64,4096]{1,0:T(8,128)(2,1)S(1)}, s32[1,1]{1,0:T(1,128)}) custom-call(bf16[64,4096]{1,0:T(8,128)(2,1)} %x_ref.1, s32[256,128]{1,0:T(8,128)} %bitcast.29, s32[1,8]{1,0:T(1,128)} %lab_ref.1), custom_call_target="tpu_custom_call" | custom-call | tf_op jit(solution)/shard_map/pallas_call | solution.py:618
  89.8 0.2 conditional.1
  90.1 0.8 copy.13
